TPU v7x, 32 devices: a whole 2x2x4 slice. The times are simulated.
32 devices in a mesh: dp: 16 (over z, y, x), head: 2 (over core).
Axes of the slice: x: 2, y: 2, z: 4, core: 2. Of those that a mesh axis runs over, the one named last changes fastest.
Arguments:
- hidden_in: bfloat16 [32768, 768], P('dp'), may hold values from -6 to 6
- lengths: int32 [32, 8], P('dp'), may hold values from 1 to 512, 1024 in all within a row
- buckets: int32 [2047], replicated, may hold values from 0 to 31, as said below
- gain_attn: float32 [768], replicated, may hold values from 0.5 to 1.5
- gain_ffn: float32 [768], replicated, may hold values from 0.5 to 1.5
- w_query: bfloat16 [768, 768], P(None, 'head'), may hold values from -0.02734375 to 0.02734375
- w_key: bfloat16 [768, 768], P(None, 'head'), may hold values from -0.21875 to 0.21875
- w_value: bfloat16 [768, 768], P(None, 'head'), may hold values from -0.21875 to 0.21875
- w_attn_out: bfloat16 [768, 768], P('head'), may hold values from -0.875 to 0.875
- w_in: bfloat16 [768, 3072], P(None, 'head'), may hold values from -0.21875 to 0.21875
- w_ffn_out: bfloat16 [3072, 768], P('head'), may hold values from -0.109375 to 0.109375
- rel_bias: float32 [32, 12], P(None, 'head'), may hold values from -4 to 4
- out_grad: bfloat16 [32768, 768], P(('dp', 'head'))
- adapter_weights: float32 [2512], replicated, may hold values from -4 to 4
- first_moment: float32 [2512], replicated
- second_moment: float32 [2512], replicated, as said below
- ema_weights: float32 [2512], replicated, may hold values from -4 to 4
Outputs:
- layer_out: float32 [32768, 768], P(('dp', 'head'))
- grad_in: float32 [32768, 768], P(('dp', 'head'))
- new_weights: float32 [2512], replicated
- new_first: float32 [2512], replicated
- new_second: float32 [2512], replicated
- new_ema: float32 [2512], replicated
Inputs may be any that keep to these rules, and one draw needn't show every extreme that they name: For keys before the query the bucket is below 16, for keys after it 32 / 2 or more, offset 0 has bucket 0; buckets never fall with distance on either side; the largest distance on each side has the highest bucket of that side. Each row's 8 lengths sum to 1024. `second_moment`: every entry is positive.
All inputs are finite; a program needn't handle non-finite values.
Results may differ from a plain program's by a relative error of at most 0.02.
Values may be sent and summed in bfloat16 or wider, within the bound.
No kernel may reach another device: no remote copies, remote signals or barrier semaphores. Data moves between devices by JAX's collectives and lax.ppermute only.
A program may use at most 320 MiB of HBM per device.

v0:
```python
import functools

import jax
import jax.numpy as jnp
from jax import lax
from jax.experimental import pallas as pl
from jax.experimental.pallas import tpu as pltpu
from jax.sharding import PartitionSpec as P

D = 768
DH = 64
KRON = 4
BOTTLE = 48
SEQ = 1024
MOST = 512
STEP = 10
QB = 256
KB = 256
NQ = SEQ // QB
PAIR = 2 * DH
FCHUNK = 1024
REACH = QB + MOST - 128
SPREAD = REACH + MOST + QB
CODES = SPREAD + 128
VMEM_BYTES = 127 * 2**19

eps_norm = 1e-06
beta_one = 0.9
beta_two = 0.999
adam_eps = 1e-08
learn_rate = 0.6
weight_decay = 0.01
ema_decay = 0.9
masked_score = -1e30
log2_e = 1.4426950408889634
highest = lax.Precision.HIGHEST
f32 = jnp.float32
bf16 = jnp.bfloat16


def nn(left, right):
    return lax.dot_general(left, right, (((1,), (0,)), ((), ())), preferred_element_type=f32)


def nt(left, right):
    return lax.dot_general(left, right, (((1,), (1,)), ((), ())), preferred_element_type=f32)


def tn(left, right):
    return lax.dot_general(left, right, (((0,), (0,)), ((), ())), preferred_element_type=f32)


def row_plan(len_ref, own):
    docs = len_ref.shape[1]
    sizes = [len_ref[own, doc] for doc in range(docs)]
    longest, chosen = sizes[0], jnp.int32(0)
    for doc in range(1, docs):
        longer = sizes[doc] > longest
        chosen = jnp.where(longer, doc, chosen)
        longest = jnp.maximum(longest, sizes[doc])
    start = jnp.int32(0)
    for doc in range(docs):
        start = start + jnp.where(doc < chosen, sizes[doc], 0)
    ends, total = [], jnp.int32(0)
    for doc in range(docs):
        total = total + len_ref[own, lax.rem(chosen + doc, docs)]
        ends.append(total)
    return start, ends


def key_span(ends, first_row, last_row):
    begin, finish = jnp.int32(0), jnp.int32(SEQ)
    for end in ends:
        begin = jnp.where(end <= first_row, end, begin)
    for end in reversed(ends):
        finish = jnp.where(end > last_row, end, finish)
    return lax.div(begin, KB), lax.div(finish + (KB - 1), KB)


def rotate_rows(source_ref, target_ref, shift):
    groups = SEQ // 8
    fine, coarse = shift & 7, shift >> 3
    back = (8 - fine) & 7
    keep = lax.broadcasted_iota(jnp.int32, (8, target_ref.shape[1]), 0) < 8 - fine

    def turned(group):
        rows = source_ref[pl.ds(pl.multiple_of((group & (groups - 1)) * 8, 16), 16), :].astype(f32)
        return pltpu.roll(rows[0:8], back, 0), pltpu.roll(rows[8:16], back, 0)

    def some(part, carry):
        first, second = carry
        for pair in range(4):
            group = part * 8 + pair * 2
            third, fourth = turned(group + 2)
            for place, left, right in ((0, first, second), (1, second, third)):
                to = ((group + place - coarse) & (groups - 1)) * 8
                target_ref[pl.ds(pl.multiple_of(to, 8), 8), :] = jnp.where(keep, left, right)
            first, second = third, fourth
        return first, second

    lax.fori_loop(0, groups // 8, some, turned(jnp.int32(0)))


def rotate_pieces(source_ref, target_ref, shift, pieces, ready):
    groups = SEQ // 8
    fine, coarse = shift & 7, shift >> 3
    back = (8 - fine) & 7
    keep = lax.broadcasted_iota(jnp.int32, (8, target_ref.shape[1]), 0) < 8 - fine

    def turned(group):
        rows = source_ref[pl.ds(pl.multiple_of(((group + coarse) & (groups - 1)) * 8, 8), 8), :]
        return pltpu.roll(rows, back, 0)

    def some(part, before):
        for place in range(8):
            group = part * 8 + place
            after = turned(group + 1)
            target_ref[pl.ds(pl.multiple_of(group * 8, 8), 8), :] = jnp.where(keep, before, after)
            before = after
        return before

    steps = groups // 8 // pieces
    carry = turned(jnp.int32(0))
    for piece in range(pieces):
        carry = lax.fori_loop(piece * steps, piece * steps + steps, some, carry)
        ready(piece)


def one_head(pair, half):
    lane = lax.broadcasted_iota(jnp.int32, pair.shape, 1)
    keep = lane < DH if half == 0 else lane >= DH
    return jnp.where(keep, pair, jnp.zeros_like(pair))


def flip_lanes(value):
    tiles = value.shape[1] // 128
    row = lax.broadcasted_iota(jnp.int32, (128, 128), 0)
    lane = lax.broadcasted_iota(jnp.int32, (128, 128), 1)
    stacked = jnp.concatenate([value[:, tile * 128 : tile * 128 + 128] for tile in range(tiles)], axis=0)
    flipped = exact(stacked, (row + lane == 127).astype(f32))
    return jnp.concatenate([flipped[tile * 8 : tile * 8 + 8, :] for tile in reversed(range(tiles))], axis=1)


def exact(left, right):
    return lax.dot_general(
        left, right, (((1,), (0,)), ((), ())), precision=highest, preferred_element_type=f32
    )


def bias_bands(buckets_ref, table_ref, bias_ref, lead):
    heads = table_ref.shape[0]
    top = REACH + 128 + SEQ - 1
    codes = buckets_ref[...].reshape(1, 2 * SEQ - 1)[:, top - CODES + 1 : top + 1]
    bucket = lax.broadcasted_iota(jnp.int32, (table_ref.shape[1], CODES), 0)
    per_head = exact(table_ref[...] * log2_e, (bucket == codes).astype(f32))
    per_head = flip_lanes(jnp.concatenate([per_head, jnp.zeros((8 - heads, CODES), f32)], axis=0))
    for head in range(heads):
        spread = jnp.broadcast_to(per_head[head : head + 1, :], (128, CODES))
        spread = pltpu.roll(spread, CODES - 128, 1, stride=1, stride_axis=0)
        bias_ref[lead + head] = spread[:, :SPREAD]


def places(first, width):
    return pl.ds(pl.multiple_of(first, width), width)


def key_window(ends, first_row, last_row):
    begin, finish = key_span(ends, first_row, last_row)
    wide = finish - begin > MOST // KB
    return jnp.where(wide, 0, jnp.minimum(begin, (SEQ - MOST) // KB)), wide


def pack_kernel(own_ref, len_ref, x_hbm, grad_hbm, packed_hbm, packed_grad_hbm, x_ref, grad_ref, turned_ref, sems):
    start, _ = row_plan(len_ref, own_ref[0])
    rows = pl.ds(pl.multiple_of(own_ref[0] * SEQ, SEQ), SEQ)
    loads = [
        pltpu.make_async_copy(x_hbm.at[rows, :], x_ref, sems.at[0]),
        pltpu.make_async_copy(grad_hbm, grad_ref, sems.at[1]),
    ]
    stores = [
        pltpu.make_async_copy(x_ref, packed_hbm, sems.at[2]),
        pltpu.make_async_copy(grad_ref, packed_grad_hbm, sems.at[3]),
    ]
    for load in loads:
        load.start()
    for load, store, ref in zip(loads, stores, (x_ref, grad_ref)):
        load.wait()
        rotate_rows(ref, turned_ref, start)
        ref[...] = turned_ref[...].astype(bf16)
        store.start()
    for store in stores:
        store.wait()


def pack(own, lengths, x, out_grad):
    any_space = pl.BlockSpec(memory_space=pl.ANY)
    smem = pl.BlockSpec(memory_space=pltpu.SMEM)
    return pl.pallas_call(
        pack_kernel,
        in_specs=[smem, smem, any_space, any_space],
        out_specs=[any_space, any_space],
        out_shape=[jax.ShapeDtypeStruct((SEQ, D), bf16)] * 2,
        scratch_shapes=[
            pltpu.VMEM((SEQ, D), bf16),
            pltpu.VMEM((SEQ, D), bf16),
            pltpu.VMEM((SEQ, D), f32),
            pltpu.SemaphoreType.DMA((4,)),
        ],
        compiler_params=pltpu.CompilerParams(vmem_limit_bytes=VMEM_BYTES),
        cost_estimate=pl.CostEstimate(flops=3 * 10**9, bytes_accessed=6 * 10**6, transcendentals=0),
        name="pack_rows",
    )(own, lengths, x, out_grad)


def attention_kernel(
    own_ref,
    len_ref,
    x_hbm,
    wq_own,
    wk_own,
    wv_own,
    wq_other,
    wk_other,
    wv_other,
    table_hbm,
    gain_ref,
    buckets_ref,
    table_own,
    prob_hbm,
    q_hbm,
    k_hbm,
    v_hbm,
    ctx_hbm,
    shrink_hbm,
    x_ref,
    w_ref,
    qkv_ref,
    vt_ref,
    ctx_ref,
    shrink_ref,
    table_other,
    bias_ref,
    dk_ref,
    dq_ref,
    prob_ref,
    prob_sems,
    ctx_sems,
    sems,
):
    heads = table_own.shape[0]
    half = heads * DH
    sources = (wq_own, wq_other, wk_own, wk_other, wv_own, wv_other)
    loads = [pltpu.make_async_copy(x_hbm, x_ref, sems.at[0])]
    for place, source in enumerate(sources):
        target = w_ref.at[:, place * half : place * half + half]
        loads.append(pltpu.make_async_copy(source, target, sems.at[1 + place]))
    table_load = pltpu.make_async_copy(table_hbm, table_other, sems.at[11])
    table_load.start()
    for load in loads:
        load.start()
    _, ends = row_plan(len_ref, own_ref[0])
    row = lax.broadcasted_iota(jnp.int32, dk_ref.shape, 0)
    dk_ref[...] = sum((row >= end).astype(jnp.int32) for end in ends)
    lane = lax.broadcasted_iota(jnp.int32, dq_ref.shape, 1)
    dq_ref[...] = sum((lane >= end).astype(jnp.int32) for end in ends)
    bias_bands(buckets_ref, table_own, bias_ref, 0)
    table_load.wait()
    bias_bands(buckets_ref, table_other, bias_ref, heads)
    loads[0].wait()
    inputs = x_ref[...].astype(f32)
    scale = lax.rsqrt(jnp.mean(inputs * inputs, axis=1, keepdims=True) + eps_norm)
    x_ref[...] = (inputs * scale * gain_ref[...].reshape(1, D)).astype(bf16)
    for load in loads[1:]:
        load.wait()
    q_ref, k_ref, v_ref = (qkv_ref.at[place] for place in range(3))

    def project(place, carry):
        columns = pl.ds(pl.multiple_of(place * D, D), D)
        projected = nn(x_ref[...], w_ref[:, columns])
        qkv_ref[place] = (projected * jnp.where(place == 0, log2_e, 1.0)).astype(bf16)
        return carry

    lax.fori_loop(0, 3, project, 0)
    vt_ref[...] = v_ref[...].T
    stores = [
        pltpu.make_async_copy(q_ref, q_hbm, sems.at[7]),
        pltpu.make_async_copy(k_ref, k_hbm, sems.at[8]),
        pltpu.make_async_copy(v_ref, v_hbm, sems.at[9]),
    ]
    for store in stores:
        store.start()

    def prob_copy(it, count):
        slot, rows = lax.rem(it, 2), count * KB
        return pltpu.make_async_copy(
            prob_ref.at[slot, :, 0:rows, :],
            prob_hbm.at[lax.div(it, NQ), :, lax.rem(it, NQ), 0:rows, :],
            prob_sems.at[slot],
        )

    def ctx_copy(it):
        query_rows = pl.ds(pl.multiple_of(lax.rem(it, NQ) * QB, QB), QB)
        band = pl.ds(pl.multiple_of(lax.div(it, NQ) * half, half), half)
        return pltpu.make_async_copy(
            ctx_ref.at[band, query_rows], ctx_hbm.at[band, query_rows], ctx_sems.at[it]
        )

    def with_span(it, action):
        first_row = lax.rem(it, NQ) * QB
        begin, wide = key_window(ends, first_row, first_row + QB - 1)
        pl.when(wide)(functools.partial(action, it, begin, SEQ // KB))
        pl.when(jnp.logical_not(wide))(functools.partial(action, it, begin, MOST // KB))

    def drain(it, begin, count):
        prob_copy(it, count).wait()

    def attend(it, begin, count):
        rows = count * KB
        slot, group = lax.rem(it, 2), lax.div(it, NQ)
        first_row, first_key = lax.rem(it, NQ) * QB, pl.multiple_of(begin * KB, KB)
        key_rows = pl.ds(first_key, rows)
        query_rows = pl.ds(pl.multiple_of(first_row, QB), QB)
        doc_key = jnp.concatenate([dk_ref[key_rows, :]] * (QB // 128), axis=1)
        same = doc_key == dq_ref[0:1, query_rows]

        bands = []
        for part in range(rows // 128):
            lane = jnp.clip(first_row - first_key + (REACH - part * 128), 0, SPREAD - QB)
            bands.append(pl.ds(pl.multiple_of(lane, 128), QB))

        def some_heads(members):
            scores, totals, probs = [], [], []
            for head in members:
                lanes = places(group * half + head // 2 * PAIR, PAIR)
                scores.append(nt(k_ref[key_rows, lanes], one_head(q_ref[query_rows, lanes], len(scores) % 2)))
            for head, score in zip(members, scores):
                bias = jnp.concatenate(
                    [bias_ref[group * heads + head, :, lanes] for lanes in bands], axis=0
                )
                score = jnp.where(same, score + bias, masked_score)
                expo = jnp.exp2(score - jnp.max(score, axis=0, keepdims=True))
                totals.append(1.0 / jnp.sum(expo, axis=0, keepdims=True))
                probs.append(expo.astype(bf16))
                prob_ref[slot, head, 0:rows, :] = probs[-1]
            for head, total, prob in zip(members, totals, probs):
                band = places(group * half + head * DH, DH)
                context = nn(vt_ref[band, key_rows], prob)
                ctx_ref[band, query_rows] = (context * total).astype(bf16)
                shrink_ref[places(group * 8 + head, 1), query_rows] = total

        if rows <= MOST:
            some_heads(range(heads))
        else:

            def one_pair(pair, carry):
                some_heads((2 * pair, 2 * pair + 1))
                return carry

            lax.fori_loop(0, heads // 2, one_pair, 0)
        prob_copy(it, count).start()
        ctx_copy(it).start()

    def one_block(it, carry):
        @pl.when(it >= 2)
        def _drain():
            with_span(it - 2, drain)

        with_span(it, attend)
        return carry

    lax.fori_loop(0, 2 * NQ, one_block, 0)
    stores.append(pltpu.make_async_copy(shrink_ref, shrink_hbm, sems.at[10]))
    stores[-1].start()
    with_span(jnp.int32(2 * NQ - 2), drain)
    with_span(jnp.int32(2 * NQ - 1), drain)
    for it in range(2 * NQ):
        ctx_copy(it).wait()
    for copy in stores:
        copy.wait()


def attention_forward(own, lengths, x, weights, gain, buckets, table_own, table_other):
    heads = table_own.shape[0]
    any_space = pl.BlockSpec(memory_space=pl.ANY)
    vmem = pl.BlockSpec(memory_space=pltpu.VMEM)
    smem = pl.BlockSpec(memory_space=pltpu.SMEM)
    return pl.pallas_call(
        attention_kernel,
        in_specs=[smem, smem] + [any_space] * 8 + [vmem] * 3,
        out_specs=[any_space] * 6,
        out_shape=[
            jax.ShapeDtypeStruct((2, heads, NQ, SEQ, QB), bf16),
            jax.ShapeDtypeStruct((SEQ, D), bf16),
            jax.ShapeDtypeStruct((SEQ, D), bf16),
            jax.ShapeDtypeStruct((SEQ, D), bf16),
            jax.ShapeDtypeStruct((D, SEQ), bf16),
            jax.ShapeDtypeStruct((16, SEQ), f32),
        ],
        scratch_shapes=[
            pltpu.VMEM((SEQ, D), bf16),
            pltpu.VMEM((D, 3 * D), bf16),
            pltpu.VMEM((3, SEQ, D), bf16),
            pltpu.VMEM((D, SEQ), bf16),
            pltpu.VMEM((D, SEQ), bf16),
            pltpu.VMEM((16, SEQ), f32),
            pltpu.VMEM(table_own.shape, f32),
            pltpu.VMEM((2 * heads, 128, SPREAD), f32),
            pltpu.VMEM((SEQ, 128), jnp.int32),
            pltpu.VMEM((8, SEQ), jnp.int32),
            pltpu.VMEM((2, heads, SEQ, QB), bf16),
            pltpu.SemaphoreType.DMA((2,)),
            pltpu.SemaphoreType.DMA((2 * NQ,)),
            pltpu.SemaphoreType.DMA((12,)),
        ],
        compiler_params=pltpu.CompilerParams(vmem_limit_bytes=VMEM_BYTES),
        cost_estimate=pl.CostEstimate(flops=25 * 10**9, bytes_accessed=30 * 10**6, transcendentals=4 * 10**6),
        name="attention_forward",
    )(own, lengths, x, *weights, table_other, gain, buckets, table_own)


root_two_over_pi = 0.7978845608028654
cubic = 0.044715


def gelu_both(value):
    square = value * value
    slow = jnp.tanh(value * (root_two_over_pi + (root_two_over_pi * cubic) * square))
    half = 0.5 * value
    act = half + half * slow
    slope = (0.5 + 0.5 * slow) + half * (1.0 - slow * slow) * (
        root_two_over_pi + (3.0 * root_two_over_pi * cubic) * square
    )
    return act, slope


def block_of(index, width, blocks):
    return sum((index >= width * place).astype(jnp.int32) for place in range(1, blocks))


class Kronecker:
    def __init__(self, core, small, large, factor, swapped):
        terms, rows = KRON, KRON * KRON
        sub, leaf = BOTTLE // KRON, D // KRON
        self.factor = factor
        row = lax.broadcasted_iota(jnp.int32, (rows, rows * KRON), 0)
        item = lax.broadcasted_iota(jnp.int32, (rows, rows * KRON), 1)
        item_of = lax.broadcasted_iota(jnp.int32, (rows * KRON, BOTTLE), 0)
        lane_block = block_of(lax.broadcasted_iota(jnp.int32, (rows * KRON, BOTTLE), 1), sub, KRON)
        if swapped:
            self.holds = ((item >> 4) == (row >> 2)) & ((item & 3) == (row & 3))
            pick = ((item_of >> 2) & 3) == lane_block
        else:
            self.holds = (item >> 2) == row
            pick = (item_of & 3) == lane_block
        self.pick = pick.astype(f32)
        self.core = exact(jnp.where(self.holds, jnp.broadcast_to(core, self.holds.shape), 0.0), self.pick)
        self.small = jnp.concatenate(
            [
                jnp.broadcast_to(
                    jnp.concatenate([small[:, n * sub : n * sub + sub]] * KRON, axis=1), (KRON, BOTTLE)
                )
                for n in range(terms)
            ],
            axis=0,
        )
        large = jnp.concatenate(
            [
                jnp.broadcast_to(
                    jnp.concatenate([large[:, n * leaf : n * leaf + leaf]] * KRON, axis=1), (KRON, D)
                )
                for n in range(terms)
            ],
            axis=0,
        )
        row = lax.broadcasted_iota(jnp.int32, (rows, D), 0)
        lane = lax.broadcasted_iota(jnp.int32, (rows, D), 1)
        self.diagonal = (row & 3) == block_of(lane, leaf, KRON)
        self.large = jnp.where(self.diagonal, large, 0.0)
        self.mix = self.core * self.small

    def matrix(self):
        return exact(self.mix.T, self.large) * self.factor

    def gradient(self, grad):
        sub, leaf = BOTTLE // KRON, D // KRON
        inner = self.factor * lax.dot_general(
            self.large, grad, (((1,), (1,)), ((), ())), preferred_element_type=f32
        )
        core = lax.dot_general(
            self.small * inner, self.pick, (((1,), (1,)), ((), ())), preferred_element_type=f32
        )
        core = jnp.sum(jnp.where(self.holds, core, 0.0), axis=0, keepdims=True)
        by_term = self.core * inner
        outer = self.factor * jnp.where(self.diagonal, nn(self.mix, grad), 0.0)
        small, large = [], []
        for n in range(KRON):
            row = jnp.sum(by_term[n * KRON : n * KRON + KRON, :], axis=0, keepdims=True)
            small.append(sum(row[:, b * sub : b * sub + sub] for b in range(KRON)))
            row = jnp.sum(outer[n * KRON : n * KRON + KRON, :], axis=0, keepdims=True)
            large.append(sum(row[:, a * leaf : a * leaf + leaf] for a in range(KRON)))
        return core, jnp.concatenate(small, axis=1), jnp.concatenate(large, axis=1)


def both_adapters(flat):
    widths = (KRON * KRON * KRON, D, BOTTLE, BOTTLE, D, BOTTLE, D)
    pieces, place = [], 0
    for width in widths:
        pieces.append(flat[:, place : place + width])
        place = place + width
    core, down_left, down_right, up_left, up_right, bias_down, bias_up = pieces
    down = Kronecker(core, down_right, down_left, (KRON * D) ** (-0.5), False)
    up = Kronecker(core, up_left, up_right, BOTTLE ** (-0.5), True)
    return down, up, bias_down, bias_up


def feed_forward_kernel(
    own_ref,
    len_ref,
    prob_hbm,
    q_hbm,
    k_hbm,
    v_hbm,
    ctx_hbm,
    shrink_hbm,
    x_hbm,
    grad_hbm,
    wo_own,
    wo_other,
    win_own,
    win_other,
    wout_own,
    wout_other,
    wq_own,
    wk_own,
    wv_own,
    wq_other,
    wk_other,
    wv_other,
    gain_attn_ref,
    gain_ffn_ref,
    flat_ref,
    out_hbm,
    grad_in_hbm,
    flat_grad_ref,
    ctx_ref,
    x_ref,
    grad_ref,
    wo_ref,
    win_ref,
    wout_ref,
    slope_ref,
    res_ref,
    res_grad_ref,
    delta_ref,
    shrink_ref,
    dqt_ref,
    sums_ref,
    low_ref,
    prob_ref,
    prob_sems,
    sems,
):
    start, ends = row_plan(len_ref, own_ref[0])
    half = wo_own.shape[0]
    hidden = win_own.shape[1]
    heads = half // DH
    chunks = 2 * hidden // FCHUNK

    def load(source, target, place):
        return pltpu.make_async_copy(source, target, sems.at[place])

    first = [
        load(ctx_hbm, ctx_ref, 0),
        load(wo_own, wo_ref.at[0:half, :], 1),
        load(wo_other, wo_ref.at[half : 2 * half, :], 2),
        load(x_hbm, x_ref, 3),
    ]
    ffn_loads = [
        load(win_own, win_ref.at[:, 0:hidden], 4),
        load(wout_own, wout_ref.at[0:hidden, :], 5),
        load(win_other, win_ref.at[:, hidden : 2 * hidden], 6),
        load(wout_other, wout_ref.at[hidden : 2 * hidden, :], 7),
    ]
    base = 10
    grad_load = load(grad_hbm, grad_ref, base)
    v_ref, k_ref, q_ref = (wout_ref.at[place * SEQ : place * SEQ + SEQ, :] for place in range(3))
    late = [
        load(v_hbm, v_ref, base + 1),
        load(k_hbm, k_ref, base + 3),
        load(q_hbm, q_ref, base + 2),
    ]
    shrink_load = load(shrink_hbm, shrink_ref, base + 4)
    out_copy = load(res_grad_ref, out_hbm, base + 5)
    out_pieces = [
        load(
            res_ref.at[piece * QB : piece * QB + QB, :], grad_in_hbm.at[piece * QB : piece * QB + QB, :], piece
        )
        for piece in range(NQ)
    ]
    qkv_loads = [
        load(source, win_ref.at[:, place * half : place * half + half], 4 + place)
        for place, source in enumerate((wq_own, wq_other, wk_own, wk_other, wv_own, wv_other))
    ]
    for copy in first:
        copy.start()
    for copy in ffn_loads:
        copy.start()
    grad_load.start()
    shrink_load.start()

    def prob_copy(it, count):
        slot, rows = lax.rem(it, 2), count * KB
        return pltpu.make_async_copy(
            prob_hbm.at[lax.div(it, NQ), :, lax.rem(it, NQ), 0:rows, :],
            prob_ref.at[slot, :, 0:rows, :],
            prob_sems.at[slot],
        )

    def with_span(it, action):
        first_row = lax.rem(it, NQ) * QB
        _, wide = key_window(ends, first_row, first_row + QB - 1)
        pl.when(wide)(functools.partial(action, it, SEQ // KB))
        pl.when(jnp.logical_not(wide))(functools.partial(action, it, MOST // KB))

    def fetch(it, count):
        prob_copy(it, count).start()

    def arrive(it, count):
        prob_copy(it, count).wait()

    with_span(jnp.int32(0), fetch)
    flat = flat_ref[...].reshape(1, flat_ref.shape[0])
    down_maker, up_maker, bias_down, bias_up = both_adapters(flat)
    down, up = down_maker.matrix().astype(bf16), up_maker.matrix().astype(bf16)
    gain = gain_ffn_ref[...].reshape(1, D)
    for copy in first:
        copy.wait()
    residual = x_ref[...].astype(f32) + tn(ctx_ref[...], wo_ref[...])
    res_ref[...] = residual
    scale = lax.rsqrt(jnp.mean(residual * residual, axis=1, keepdims=True) + eps_norm)
    low = (residual * scale * gain).astype(bf16)

    for copy in ffn_loads[:2]:
        copy.wait()
    low_ref[...] = low
    sums_ref[...] = jnp.zeros_like(sums_ref)

    def halves_of(chunk):
        return [places(chunk * FCHUNK + part * (FCHUNK // 2), FCHUNK // 2) for part in range(2)]

    def forward_chunk(chunk, carry):
        @pl.when(chunk == hidden // FCHUNK)
        def _other_side():
            for copy in ffn_loads[2:]:
                copy.wait()

        halves = halves_of(chunk)
        pre_acts = [nn(low_ref[...], win_ref[:, cols]) for cols in halves]
        for pre_act, cols in zip(pre_acts, halves):
            act, slope = gelu_both(pre_act)
            slope_ref[:, cols] = slope.astype(bf16)
            sums_ref[...] += nn(act.astype(bf16), wout_ref[cols, :])
        return carry

    lax.fori_loop(0, chunks, forward_chunk, 0)
    mixed = sums_ref[...]
    grad_load.wait()
    out_grad_low = grad_ref[...]
    mixed_low = mixed.astype(bf16)
    bottle, bottle_slope = gelu_both(nt(mixed_low, down) + bias_down)
    bottle_low = bottle.astype(bf16)
    sums_ref[...] = res_ref[...] + mixed + nn(bottle_low, up) + bias_up
    rotate_rows(sums_ref, res_grad_ref, SEQ - start)
    out_copy.start()
    bottle_grad = (nt(out_grad_low, up) * bottle_slope).astype(bf16)
    mixed_grad = (out_grad_low.astype(f32) + nn(bottle_grad, down)).astype(bf16)
    up_grad = tn(bottle_low, out_grad_low)
    down_grad = tn(bottle_grad, mixed_low)
    core_down, right_down, left_down = down_maker.gradient(down_grad)
    core_up, left_up, right_up = up_maker.gradient(up_grad)
    flat_grad = jnp.concatenate(
        [
            core_down + core_up,
            left_down,
            right_down,
            left_up,
            right_up,
            jnp.sum(bottle_grad.astype(f32), axis=0, keepdims=True),
            jnp.sum(out_grad_low.astype(f32), axis=0, keepdims=True),
        ],
        axis=1,
    )
    flat_grad_ref[...] = flat_grad.reshape(flat_grad_ref.shape[0])
    low_ref[...] = mixed_grad
    sums_ref[...] = jnp.zeros_like(sums_ref)

    def backward_chunk(chunk, carry):
        halves = halves_of(chunk)
        hidden_grads = [nt(low_ref[...], wout_ref[cols, :]) for cols in halves]
        for hidden_grad, cols in zip(hidden_grads, halves):
            pre_grad = (hidden_grad * slope_ref[:, cols].astype(f32)).astype(bf16)
            sums_ref[...] += nt(pre_grad, win_ref[:, cols])
        return carry

    lax.fori_loop(0, chunks, backward_chunk, 0)
    for copy in late + qkv_loads:
        copy.start()
    residual = res_ref[...]
    weighted = sums_ref[...] * gain
    inner = jnp.mean(residual * weighted, axis=1, keepdims=True)
    res_grad = grad_ref[...].astype(f32) + scale * weighted - residual * (scale * scale * scale * inner)
    out_copy.wait()
    res_grad_ref[...] = res_grad
    shrink_load.wait()
    shrink = jnp.concatenate([shrink_ref[0:heads, :], shrink_ref[8 : 8 + heads, :]], axis=0)
    shrink_top = shrink.astype(bf16)
    shrink_rest = (shrink - shrink_top.astype(f32)).astype(bf16)
    head_row = lax.broadcasted_iota(jnp.int32, (2 * heads, D), 0)
    head_lane = lax.broadcasted_iota(jnp.int32, (2 * heads, D), 1) >> 6
    spread = (head_row == head_lane).astype(bf16)
    shrink_wide = tn(shrink_top, spread) + tn(shrink_rest, spread)
    dctx = (nt(res_grad.astype(bf16), wo_ref[...]) * shrink_wide).astype(bf16)
    grad_ref[...] = dctx
    product = dctx.T.astype(f32) * ctx_ref[...].astype(f32)
    delta_ref[0 : 2 * heads, :] = jnp.sum(product.reshape(2 * heads, DH, SEQ), axis=1)
    for copy in late:
        copy.wait()
    kt_ref, dctx_ref = ctx_ref, grad_ref
    kt_ref[...] = k_ref[...].T

    def attend(it, part, carry):
        slot, group = lax.rem(it, 2), lax.div(it, NQ)
        first_row = lax.rem(it, NQ) * QB
        begin, _ = key_window(ends, first_row, first_row + QB - 1)
        key_rows = pl.ds(pl.multiple_of(begin * KB + part * MOST, KB), MOST)
        rows = pl.ds(pl.multiple_of(part * MOST, MOST), MOST)
        query_rows = pl.ds(pl.multiple_of(first_row, QB), QB)

        def lanes(pair):
            return places(group * half + pair * PAIR, PAIR)

        grads, prob_grads, score_grads, probs = [], [], [], []
        for head in range(heads):
            grads.append(one_head(dctx_ref[query_rows, lanes(head // 2)], head % 2))
            prob_grads.append(nt(v_ref[key_rows, lanes(head // 2)], grads[head]))
        for head in range(heads):
            delta = delta_ref[places(group * heads + head, 1), query_rows]
            probs.append(prob_ref[slot, head, rows, :])
            score_grads.append((probs[head].astype(f32) * (prob_grads[head] - delta)).astype(bf16))
        for pair in range(heads // 2):
            dk = dv = None
            for head in (2 * pair, 2 * pair + 1):
                band = places(group * half + head * DH, DH)
                queries = one_head(q_ref[query_rows, lanes(pair)], head % 2)
                dv_part = nn(probs[head], grads[head])
                dk_part = nn(score_grads[head], queries)
                dv = dv_part if dv is None else dv + dv_part
                dk = dk_part if dk is None else dk + dk_part
                dq = nn(kt_ref[band, key_rows], score_grads[head])
                before = jnp.where(part > 0, dqt_ref[band, query_rows].astype(f32), 0.0)
                dqt_ref[band, query_rows] = (before + dq).astype(bf16)
            sums_ref[key_rows, pair * PAIR : pair * PAIR + PAIR] += dk
            sums_ref[key_rows, half + pair * PAIR : half + pair * PAIR + PAIR] += dv
        return carry

    def one_block(it, carry):
        @pl.when(it + 1 < 2 * NQ)
        def _ahead():
            with_span(it + 1, fetch)

        with_span(it, arrive)
        first_row = lax.rem(it, NQ) * QB
        _, wide = key_window(ends, first_row, first_row + QB - 1)
        lax.fori_loop(0, jnp.where(wide, SEQ // MOST, 1), functools.partial(attend, it), 0)
        return carry

    def one_group(group, carry):
        sums_ref[...] = jnp.zeros_like(sums_ref)
        lax.fori_loop(group * NQ, group * NQ + NQ, one_block, 0)
        slope_ref[:, places((2 + group) * half, half)] = (sums_ref[:, 0:half] * (1.0 / log2_e)).astype(bf16)
        slope_ref[:, places((4 + group) * half, half)] = sums_ref[:, half : 2 * half].astype(bf16)
        return carry

    lax.fori_loop(0, 2, one_group, 0)
    slope_ref[:, 0 : 2 * half] = dqt_ref[...].T
    for copy in qkv_loads:
        copy.wait()

    def input_columns(part, carry):
        rows = pl.ds(pl.multiple_of(part * KB, KB), KB)
        sums_ref[:, rows] = nt(slope_ref[:, 0 : 6 * half], win_ref[rows, 0 : 6 * half])
        return carry

    lax.fori_loop(0, D // KB, input_columns, 0)
    normed_grad = sums_ref[...]
    inputs = x_ref[...].astype(f32)
    scale = lax.rsqrt(jnp.mean(inputs * inputs, axis=1, keepdims=True) + eps_norm)
    weighted = normed_grad * gain_attn_ref[...].reshape(1, D)
    inner = jnp.mean(inputs * weighted, axis=1, keepdims=True)
    sums_ref[...] = res_grad_ref[...] + scale * weighted - inputs * (scale * scale * scale * inner)
    rotate_pieces(sums_ref, res_ref, SEQ - start, NQ, lambda piece: out_pieces[piece].start())
    for copy in out_pieces:
        copy.wait()


def feed_forward_and_back(own, lengths, kept, x, out_grad, frozen, weights, gain_attn, gain_ffn, flat):
    any_space = pl.BlockSpec(memory_space=pl.ANY)
    vmem = pl.BlockSpec(memory_space=pltpu.VMEM)
    smem = pl.BlockSpec(memory_space=pltpu.SMEM)
    hidden = 2 * frozen[2].shape[1]
    heads = kept[0].shape[1]
    half = heads * DH
    return pl.pallas_call(
        feed_forward_kernel,
        in_specs=[smem, smem] + [any_space] * 20 + [vmem] * 3,
        out_specs=[any_space, any_space, vmem],
        out_shape=[
            jax.ShapeDtypeStruct((SEQ, D), f32),
            jax.ShapeDtypeStruct((SEQ, D), f32),
            jax.ShapeDtypeStruct(flat.shape, f32),
        ],
        scratch_shapes=[
            pltpu.VMEM((D, SEQ), bf16),
            pltpu.VMEM((SEQ, D), bf16),
            pltpu.VMEM((SEQ, D), bf16),
            pltpu.VMEM((D, D), bf16),
            pltpu.VMEM((D, hidden), bf16),
            pltpu.VMEM((hidden, D), bf16),
            pltpu.VMEM((SEQ, hidden), bf16),
            pltpu.VMEM((SEQ, D), f32),
            pltpu.VMEM((SEQ, D), f32),
            pltpu.VMEM((16, SEQ), f32),
            pltpu.VMEM((16, SEQ), f32),
            pltpu.VMEM((D, SEQ), bf16),
            pltpu.VMEM((SEQ, D), f32),
            pltpu.VMEM((SEQ, D), bf16),
            pltpu.VMEM((2, heads, SEQ, QB), bf16),
            pltpu.SemaphoreType.DMA((2,)),
            pltpu.SemaphoreType.DMA((17,)),
        ],
        compiler_params=pltpu.CompilerParams(vmem_limit_bytes=VMEM_BYTES),
        cost_estimate=pl.CostEstimate(flops=60 * 10**9, bytes_accessed=40 * 10**6, transcendentals=4 * 10**6),
        name="feed_forward_and_back",
    )(own, lengths, *kept, x, out_grad, *frozen, *weights, gain_attn, gain_ffn, flat)


def sum_everywhere(value):
    for axis in ("head", "dp"):
        size = lax.axis_size(axis)
        step = 1
        while step < size:
            value = value + lax.ppermute(value, axis, [(place, place ^ step) for place in range(size)])
            step = 2 * step
    return value


def on_device(
    hidden_in,
    lengths,
    buckets,
    gain_attn,
    gain_ffn,
    w_query,
    w_key,
    w_value,
    w_attn_out,
    w_in,
    w_ffn_out,
    rel_bias,
    out_grad,
    adapter_weights,
    first_moment,
    second_moment,
    ema_weights,
):
    swap = [(0, 1), (1, 0)]
    own = lax.axis_index("head").astype(jnp.int32).reshape(1)

    def other(value):
        return lax.ppermute(value, "head", swap)

    table = rel_bias.T
    own_qkv = (w_query, w_key, w_value)
    other_qkv = tuple(other(weight) for weight in own_qkv)
    other_table = other(table)
    rest = (w_attn_out, w_in, w_ffn_out)
    frozen = tuple(piece for weight in rest for piece in (weight, other(weight)))
    packed, packed_grad = pack(own, lengths, hidden_in, out_grad)
    kept = attention_forward(
        own, lengths, packed, own_qkv + other_qkv, gain_attn, buckets, table, other_table
    )
    layer_out, grad_in, local_grad = feed_forward_and_back(
        own, lengths, kept, packed, packed_grad, frozen, own_qkv + other_qkv, gain_attn, gain_ffn, adapter_weights
    )
    total_grad = sum_everywhere(local_grad)
    new_first = beta_one * first_moment + (1.0 - beta_one) * total_grad
    new_second = beta_two * second_moment + (1.0 - beta_two) * total_grad * total_grad
    first_hat = new_first / (1.0 - beta_one**STEP)
    second_hat = new_second / (1.0 - beta_two**STEP)
    new_weights = adapter_weights - learn_rate * (
        first_hat / (jnp.sqrt(second_hat) + adam_eps) + weight_decay * adapter_weights
    )
    new_ema = ema_decay * ema_weights + (1.0 - ema_decay) * new_weights
    return (layer_out, grad_in, new_weights, new_first, new_second, new_ema)


def solution(mesh):
    placed = (
        P("dp", None),
        P("dp", None),
        P(),
        P(),
        P(),
        P(None, "head"),
        P(None, "head"),
        P(None, "head"),
        P("head", None),
        P(None, "head"),
        P("head", None),
        P(None, "head"),
        P(("dp", "head"), None),
        P(),
        P(),
        P(),
        P(),
    )
    return jax.shard_map(
        on_device,
        mesh=mesh,
        in_specs=placed,
        out_specs=(P(("dp", "head"), None), P(("dp", "head"), None), P(), P(), P(), P()),
        check_vma=False,
    )
```

profile of v0, /device:TPU:0, one launch (start us, length us, event | category | flops | bytes accessed | tf_op | source)
XLA Modules:
  0.0 115.1 jit_solution(13488273007107895150)
XLA Ops:
  0.6 0.5 collective-permute-start
  1.2 0.1 collective-permute-start.1
  1.2 0.4 collective-permute-start.2
  1.7 0.1 collective-permute-start.3
  1.7 0.4 collective-permute-start.5
  2.2 1.6 %collective-permute-done.3.table_hbm = f32[6,32]{1,0:T(8,128)S(1)} collective-permute-done((f32[6,32]{1,0:T(8,128)}, f32[6,32]{1,0:T(8,128)S(1)}, u32[]{:S(2)}, u32[]{:S(2)}) %collective-permute-start.3) | collective-permute-done | bytes 800 | tf_op jit(solution)/shard_map/ppermute | solution.py:880
  3.8 0.1 collective-permute-start.6
  3.9 4.5 %pack_rows.1 = (bf16[1024,768]{1,0:T(8,128)(2,1)}, bf16[1024,768]{1,0:T(8,128)(2,1)}) custom-call(s32[1]{0:T(128)} %bitcast.own_ref, s32[2,8]{1,0:T(2,128)} %len_ref.5, bf16[2048,768]{1,0:T(8,128)(2,1)} %x_hbm.1, bf16[1024,768]{1,0:T(8,128)(2,1)} %grad_hbm.1), custom_call_target="tpu_custom_call" | custom-call | flops 3000000000 | bytes 6000000 | tf_op jit(solution)/shard_map/pack_rows/pallas_call | solution.py:198
  8.4 0.4 collective-permute-start.4
  8.9 25.3 %attention_forward.1 = (bf16[2,6,4,1024,256]{4,3,2,1,0:T(8,128)(2,1)}, bf16[1024,768]{1,0:T(8,128)(2,1)}, bf16[1024,768]{1,0:T(8,128)(2,1)}, bf16[1024,768]{1,0:...) custom-call(s32[1]{0:T(128)} %bitcast.own_ref, s32[2,8]{1,0:T(2,128)} %len_ref.5, ...), custom_call_target="tpu_custom_call" | custom-call | flops 24999999488 | bytes 30000000 | tf_op jit(solution)/shard_map/attention_forward/pallas_call | solution.py:387
  34.3 0.0 copy-start
  34.3 61.5 %feed_forward_and_back.1 = (f32[1024,768]{1,0:T(8,128)}, f32[1024,768]{1,0:T(8,128)}, f32[2512]{0:T(1024)}) custom-call(s32[1]{0:T(128)} %bitcast.own_ref, s32[2,8]{1,0:T(2,128)} %len_ref.5, bf16[2,6,4,1024,256]{4,3,2,1,0:T(8,128)(2,1)} %get-tuple-element.18.prob_hbm, bf16[1024,768]{1,0:T(8,128)(2,1)} %get-tuple-element.19.q_hbm, ...), custom_call_target="tpu_custom_call" | custom-call | flops 60000002048 | bytes 40000000 | tf_op jit(solution)/shard_map/feed_forward_and_back/pallas_call | solution.py:813
  95.8 0.2 collective-permute-start.7
  96.0 1.2 %collective-permute-done.7 = f32[2512]{0:T(1024)S(1)} collective-permute-done((f32[2512]{0:T(1024)}, f32[2512]{0:T(1024)S(1)}, u32[]{:S(2)}, u32[]{:S(2)}) %collective-permute-start.7) | collective-permute-done | bytes 10080 | tf_op jit(solution)/shard_map/ppermute | solution.py:852
  97.3 0.7 add.33
  98.0 2.6 %collective-permute-start.8 = (f32[2512]{0:T(1024)S(1)}, f32[2512]{0:T(1024)S(1)}, u32[]{:S(2)}, u32[]{:S(2)}) collective-permute-start(f32[2512]{0:T(1024)S(1)} %add.33), channel_id=1, source_target_pairs={{0,2},{2,0},{4,6},{6,4},{8,10},{10,8},{12,14},{14,12},{16,18},{18,... | collective-permute-start | bytes 30152 | tf_op jit(solution)/shard_map/ppermute | solution.py:852
  100.6 1.7 %collective-permute-done.8 = f32[2512]{0:T(1024)S(1)} collective-permute-done((f32[2512]{0:T(1024)S(1)}, f32[2512]{0:T(1024)S(1)}, u32[]{:S(2)}, u32[]{:S(2)}) %collective-permute-start.8) | collective-permute-done | bytes 10080 | tf_op jit(solution)/shard_map/ppermute | solution.py:852
  102.3 2.1 %collective-permute-start.9 = (f32[2512]{0:T(1024)S(1)}, f32[2512]{0:T(1024)S(1)}, u32[]{:S(2)}, u32[]{:S(2)}) collective-permute-start(f32[2512]{0:T(1024)S(1)} %add.34), channel_id=1, source_target_pairs={{0,4},{2,6},{4,0},{6,2},{8,12},{10,14},{12,8},{14,10},{16,20},{18,... | collective-permute-start | bytes 30152 | tf_op jit(solution)/shard_map/ppermute | solution.py:852
  104.3 1.7 %collective-permute-done.9 = f32[2512]{0:T(1024)S(1)} collective-permute-done((f32[2512]{0:T(1024)S(1)}, f32[2512]{0:T(1024)S(1)}, u32[]{:S(2)}, u32[]{:S(2)}) %collective-permute-start.9) | collective-permute-done | bytes 10080 | tf_op jit(solution)/shard_map/ppermute | solution.py:852
  106.0 2.1 %collective-permute-start.10 = (f32[2512]{0:T(1024)S(1)}, f32[2512]{0:T(1024)S(1)}, u32[]{:S(2)}, u32[]{:S(2)}) collective-permute-start(f32[2512]{0:T(1024)S(1)} %add.35), channel_id=1, source_target_pairs={{0,8},{2,10},{4,12},{6,14},{8,0},{10,2},{12,4},{14,6},{16,24},{18,... | collective-permute-start | bytes 30152 | tf_op jit(solution)/shard_map/ppermute | solution.py:852
  108.1 1.7 %collective-permute-done.10 = f32[2512]{0:T(1024)S(1)} collective-permute-done((f32[2512]{0:T(1024)S(1)}, f32[2512]{0:T(1024)S(1)}, u32[]{:S(2)}, u32[]{:S(2)}) %collective-permute-start.10) | collective-permute-done | bytes 10080 | tf_op jit(solution)/shard_map/ppermute | solution.py:852
  109.8 3.0 %collective-permute-start.11 = (f32[2512]{0:T(1024)S(1)}, f32[2512]{0:T(1024)S(1)}, u32[]{:S(2)}, u32[]{:S(2)}) collective-permute-start(f32[2512]{0:T(1024)S(1)} %add.36), channel_id=1, source_target_pairs={{0,16},{2,18},{4,20},{6,22},{8,24},{10,26},{12,28},{14,30},{16,0},... | collective-permute-start | bytes 30152 | tf_op jit(solution)/shard_map/ppermute | solution.py:852
  112.8 1.7 %collective-permute-done.11 = f32[2512]{0:T(1024)S(1)} collective-permute-done((f32[2512]{0:T(1024)S(1)}, f32[2512]{0:T(1024)S(1)}, u32[]{:S(2)}, u32[]{:S(2)}) %collective-permute-start.11) | collective-permute-done | bytes 10080 | tf_op jit(solution)/shard_map/ppermute | solution.py:852
  114.5 0.6 multiply_add_fusion
  (18 shorter events, 0.1 us)
Async XLA Ops:
  0.6 7.8 %collective-permute-start = (bf16[768,384]{1,0:T(8,128)(2,1)}, bf16[768,384]{1,0:T(8,128)(2,1)}, u32[]{:S(2)}, u32[]{:S(2)}) collective-permute-start(bf16[768,384]{1,0:T(8,128)(2,1)} %wq_own.3), channel_id=1, source_target_pairs={{0,1},{1,0},{2,3},{3,2},{4,5},{5,4},{6,7},{7,6},{8,9},{9,8},{10,11... | collective-permute-start | bytes 1769480 | tf_op jit(solution)/shard_map/ppermute | solution.py:880
  1.2 7.7 %collective-permute-start.1 = (bf16[768,384]{1,0:T(8,128)(2,1)}, bf16[768,384]{1,0:T(8,128)(2,1)}, u32[]{:S(2)}, u32[]{:S(2)}) collective-permute-start(bf16[768,384]{1,0:T(8,128)(2,1)} %wk_own.3), channel_id=1, source_target_pairs={{0,1},{1,0},{2,3},{3,2},{4,5},{5,4},{6,7},{7,6},{8,9},{9,8},{10,11... | collective-permute-start | bytes 1769480 | tf_op jit(solution)/shard_map/ppermute | solution.py:880
  1.2 7.6 %collective-permute-start.2 = (bf16[768,384]{1,0:T(8,128)(2,1)}, bf16[768,384]{1,0:T(8,128)(2,1)}, u32[]{:S(2)}, u32[]{:S(2)}) collective-permute-start(bf16[768,384]{1,0:T(8,128)(2,1)} %wv_own.3), channel_id=1, source_target_pairs={{0,1},{1,0},{2,3},{3,2},{4,5},{5,4},{6,7},{7,6},{8,9},{9,8},{10,11... | collective-permute-start | bytes 1769480 | tf_op jit(solution)/shard_map/ppermute | solution.py:880
  1.7 2.1 %collective-permute-start.3 = (f32[6,32]{1,0:T(8,128)}, f32[6,32]{1,0:T(8,128)S(1)}, u32[]{:S(2)}, u32[]{:S(2)}) collective-permute-start(f32[6,32]{1,0:T(8,128)} %bitcast.2), channel_id=1, source_target_pairs={{0,1},{1,0},{2,3},{3,2},{4,5},{5,4},{6,7},{7,6},{8,9},{9,8},{10,11... | collective-permute-start | bytes 2312 | tf_op jit(solution)/shard_map/ppermute | solution.py:880
  1.7 32.5 %collective-permute-start.5 = (bf16[768,1536]{1,0:T(8,128)(2,1)}, bf16[768,1536]{1,0:T(8,128)(2,1)}, u32[]{:S(2)}, u32[]{:S(2)}) collective-permute-start(bf16[768,1536]{1,0:T(8,128)(2,1)} %win_own.1), channel_id=1, source_target_pairs={{0,1},{1,0},{2,3},{3,2},{4,5},{5,4},{6,7},{7,6},{8,9},{9,8},{10,11... | collective-permute-start | bytes 7077896 | tf_op jit(solution)/shard_map/ppermute | solution.py:880
  3.8 4.6 %copy-start.4 = (f32[6,32]{1,0:T(8,128)}, f32[6,32]{1,0:T(8,128)S(1)}, u32[]{:S(2)}) copy-start(f32[6,32]{1,0:T(8,128)S(1)} %collective-permute-done.3.table_hbm) | copy-start | bytes 2308
  3.8 30.5 %collective-permute-start.6 = (bf16[1536,768]{1,0:T(8,128)(2,1)}, bf16[1536,768]{1,0:T(8,128)(2,1)}, u32[]{:S(2)}, u32[]{:S(2)}) collective-permute-start(bf16[1536,768]{1,0:T(8,128)(2,1)} %wout_own.1), channel_id=1, source_target_pairs={{0,1},{1,0},{2,3},{3,2},{4,5},{5,4},{6,7},{7,6},{8,9},{9,8},{10,11... | collective-permute-start | bytes 7077896 | tf_op jit(solution)/shard_map/ppermute | solution.py:880
  8.4 25.8 %collective-permute-start.4 = (bf16[384,768]{1,0:T(8,128)(2,1)}, bf16[384,768]{1,0:T(8,128)(2,1)}, u32[]{:S(2)}, u32[]{:S(2)}) collective-permute-start(bf16[384,768]{1,0:T(8,128)(2,1)} %wo_own.1), channel_id=1, source_target_pairs={{0,1},{1,0},{2,3},{3,2},{4,5},{5,4},{6,7},{7,6},{8,9},{9,8},{10,11... | collective-permute-start | bytes 1769480 | tf_op jit(solution)/shard_map/ppermute | solution.py:880
  34.3 80.2 %copy-start = (f32[2512]{0:T(1024)S(1)}, f32[2512]{0:T(1024)}, u32[]{:S(2)}) copy-start(f32[2512]{0:T(1024)} %flat_ref.1) | copy-start | bytes 30148
  34.3 80.2 %copy-start.1 = (f32[2512]{0:T(1024)S(1)}, f32[2512]{0:T(1024)}, u32[]{:S(2)}) copy-start(f32[2512]{0:T(1024)} %param.33) | copy-start | bytes 30148
  34.3 80.2 %copy-start.2 = (f32[2512]{0:T(1024)S(1)}, f32[2512]{0:T(1024)}, u32[]{:S(2)}) copy-start(f32[2512]{0:T(1024)} %param.31) | copy-start | bytes 30148
  34.3 80.2 %copy-start.3 = (f32[2512]{0:T(1024)S(1)}, f32[2512]{0:T(1024)}, u32[]{:S(2)}) copy-start(f32[2512]{0:T(1024)} %param.32) | copy-start | bytes 30148
  95.8 1.5 %collective-permute-start.7 = (f32[2512]{0:T(1024)}, f32[2512]{0:T(1024)S(1)}, u32[]{:S(2)}, u32[]{:S(2)}) collective-permute-start(f32[2512]{0:T(1024)} %get-tuple-element.27), channel_id=1, source_target_pairs={{0,1},{1,0},{2,3},{3,2},{4,5},{5,4},{6,7},{7,6},{8,9},{9,8},{10,11... | collective-permute-start | bytes 30152 | tf_op jit(solution)/shard_map/ppermute | solution.py:852
  98.0 4.3 %collective-permute-start.8 = (f32[2512]{0:T(1024)S(1)}, f32[2512]{0:T(1024)S(1)}, u32[]{:S(2)}, u32[]{:S(2)}) collective-permute-start(f32[2512]{0:T(1024)S(1)} %add.33), channel_id=1, source_target_pairs={{0,2},{2,0},{4,6},{6,4},{8,10},{10,8},{12,14},{14,12},{16,18},{18,... | collective-permute-start | bytes 30152 | tf_op jit(solution)/shard_map/ppermute | solution.py:852
  102.3 3.7 %collective-permute-start.9 = (f32[2512]{0:T(1024)S(1)}, f32[2512]{0:T(1024)S(1)}, u32[]{:S(2)}, u32[]{:S(2)}) collective-permute-start(f32[2512]{0:T(1024)S(1)} %add.34), channel_id=1, source_target_pairs={{0,4},{2,6},{4,0},{6,2},{8,12},{10,14},{12,8},{14,10},{16,20},{18,... | collective-permute-start | bytes 30152 | tf_op jit(solution)/shard_map/ppermute | solution.py:852
  106.0 3.8 %collective-permute-start.10 = (f32[2512]{0:T(1024)S(1)}, f32[2512]{0:T(1024)S(1)}, u32[]{:S(2)}, u32[]{:S(2)}) collective-permute-start(f32[2512]{0:T(1024)S(1)} %add.35), channel_id=1, source_target_pairs={{0,8},{2,10},{4,12},{6,14},{8,0},{10,2},{12,4},{14,6},{16,24},{18,... | collective-permute-start | bytes 30152 | tf_op jit(solution)/shard_map/ppermute | solution.py:852
  109.8 4.7 %collective-permute-start.11 = (f32[2512]{0:T(1024)S(1)}, f32[2512]{0:T(1024)S(1)}, u32[]{:S(2)}, u32[]{:S(2)}) collective-permute-start(f32[2512]{0:T(1024)S(1)} %add.36), channel_id=1, source_target_pairs={{0,16},{2,18},{4,20},{6,22},{8,24},{10,26},{12,28},{14,30},{16,0},... | collective-permute-start | bytes 30152 | tf_op jit(solution)/shard_map/ppermute | solution.py:852
where the time goes:
time: 115 us
  Pallas kernels  91.4 us (79%)
  starting transfers between devices  12.1 us (11%)
  waiting for transfers between devices  9.55 us (8%)
  other arithmetic  1.36 us (1%)
    pallas_call x1, Pallas kernels, feed_forward_and_back(): pl.pallas_call(feed_forward_kernel, in_specs=[smem, smem] + [any_space] *...  61.5 us
    pallas_call x1, Pallas kernels, attention_forward(): pl.pallas_call(attention_kernel, in_specs=[smem, smem] + [any_space] * 8...  25.3 us
    ppermute x5, starting transfers between devices, sum_everywhere(): lax.ppermute(value, axis, [(place, place ^ step) for place in range(size)])  9.97 us
    ppermute x5, waiting for transfers between devices, sum_everywhere(): lax.ppermute(value, axis, [(place, place ^ step) for place in range(size)])  7.94 us
    pallas_call x1, Pallas kernels, pack(): pl.pallas_call(pack_kernel, in_specs=[smem, smem, any_space, any_space],...  4.5 us
  transfers between devices with their start and end apart: 12, of which 6 were waited for; matrix products, arithmetic and copies ran while one was open for 0% of the time, Pallas kernels for 26%

commit v1 on v0

--- a/solution.py
+++ b/solution.py
@@ -147,17 +147,20 @@
     )
 
 
-def bias_bands(buckets_ref, table_ref, bias_ref, lead):
+def bias_rows(buckets_ref, table_ref, rows_ref, lead):
     heads = table_ref.shape[0]
     top = REACH + 128 + SEQ - 1
     codes = buckets_ref[...].reshape(1, 2 * SEQ - 1)[:, top - CODES + 1 : top + 1]
     bucket = lax.broadcasted_iota(jnp.int32, (table_ref.shape[1], CODES), 0)
     per_head = exact(table_ref[...] * log2_e, (bucket == codes).astype(f32))
     per_head = flip_lanes(jnp.concatenate([per_head, jnp.zeros((8 - heads, CODES), f32)], axis=0))
-    for head in range(heads):
-        spread = jnp.broadcast_to(per_head[head : head + 1, :], (128, CODES))
-        spread = pltpu.roll(spread, CODES - 128, 1, stride=1, stride_axis=0)
-        bias_ref[lead + head] = spread[:, :SPREAD]
+    rows_ref[lead : lead + heads, :] = per_head[0:heads, :]
+
+
+def bias_band(rows_ref, bias_ref, head):
+    spread = jnp.broadcast_to(rows_ref[pl.ds(head, 1), :], (128, CODES))
+    spread = pltpu.roll(spread, CODES - 128, 1, stride=1, stride_axis=0)
+    bias_ref[head] = spread[:, :SPREAD]
 
 
 def places(first, width):
@@ -239,6 +242,7 @@
     ctx_ref,
     shrink_ref,
     table_other,
+    rows_ref,
     bias_ref,
     dk_ref,
     dq_ref,
@@ -263,20 +267,27 @@
     dk_ref[...] = sum((row >= end).astype(jnp.int32) for end in ends)
     lane = lax.broadcasted_iota(jnp.int32, dq_ref.shape, 1)
     dq_ref[...] = sum((lane >= end).astype(jnp.int32) for end in ends)
-    bias_bands(buckets_ref, table_own, bias_ref, 0)
+    bias_rows(buckets_ref, table_own, rows_ref, 0)
     table_load.wait()
-    bias_bands(buckets_ref, table_other, bias_ref, heads)
+    bias_rows(buckets_ref, table_other, rows_ref, heads)
     loads[0].wait()
     inputs = x_ref[...].astype(f32)
     scale = lax.rsqrt(jnp.mean(inputs * inputs, axis=1, keepdims=True) + eps_norm)
     x_ref[...] = (inputs * scale * gain_ref[...].reshape(1, D)).astype(bf16)
-    for load in loads[1:]:
-        load.wait()
     q_ref, k_ref, v_ref = (qkv_ref.at[place] for place in range(3))
 
     def project(place, carry):
+        for part in range(3):
+
+            @pl.when(place == part)
+            def _arrive():
+                loads[1 + 2 * part].wait()
+                loads[2 + 2 * part].wait()
+
         columns = pl.ds(pl.multiple_of(place * D, D), D)
         projected = nn(x_ref[...], w_ref[:, columns])
+        for head in range(2 * heads // 3):
+            bias_band(rows_ref, bias_ref, place * (2 * heads // 3) + head)
         qkv_ref[place] = (projected * jnp.where(place == 0, log2_e, 1.0)).astype(bf16)
         return carry
 
@@ -404,6 +415,7 @@
             pltpu.VMEM((D, SEQ), bf16),
             pltpu.VMEM((16, SEQ), f32),
             pltpu.VMEM(table_own.shape, f32),
+            pltpu.VMEM((16, CODES), f32),
             pltpu.VMEM((2 * heads, 128, SPREAD), f32),
             pltpu.VMEM((SEQ, 128), jnp.int32),
             pltpu.VMEM((8, SEQ), jnp.int32),
@@ -883,9 +895,9 @@
     own_qkv = (w_query, w_key, w_value)
     other_qkv = tuple(other(weight) for weight in own_qkv)
     other_table = other(table)
-    rest = (w_attn_out, w_in, w_ffn_out)
+    packed, packed_grad = pack(own, lengths, hidden_in, out_grad)
+    rest = lax.optimization_barrier((w_attn_out, w_in, w_ffn_out, packed))[:3]
     frozen = tuple(piece for weight in rest for piece in (weight, other(weight)))
-    packed, packed_grad = pack(own, lengths, hidden_in, out_grad)
     kept = attention_forward(
         own, lengths, packed, own_qkv + other_qkv, gain_attn, buckets, table, other_table
     )

time: 115 us -> 111 us (0.965)
  Pallas kernels: 91.4 us -> 88.8 us
  waiting for transfers between devices: 9.55 us -> 8.01 us
    pallas_call x1, Pallas kernels: 25.3 us -> 22.8 us  [attention_forward(): pl.pallas_call(attention_kernel, in_specs=[smem, smem] + [any_space] * 8...]
    ppermute x7, waiting for transfers between devices: 1.61 us -> 0.02 us  [other(): return lax.ppermute(value, 'head', swap)]
  transfers between devices with their start and end apart: 12 -> 12, of which waited for: 6 -> 5; matrix products, arithmetic and copies ran while one was open for 0% -> 0% of each run, Pallas kernels for 26% -> 25%
where the time goes in v1:
time: 111 us
  Pallas kernels  88.8 us (80%)
  starting transfers between devices  12.1 us (11%)
  waiting for transfers between devices  8.01 us (7%)
  other arithmetic  1.36 us (1%)
    pallas_call x1, Pallas kernels, feed_forward_and_back(): pl.pallas_call(feed_forward_kernel, in_specs=[smem, smem] + [any_space] *...  61.5 us
    pallas_call x1, Pallas kernels, attention_forward(): pl.pallas_call(attention_kernel, in_specs=[smem, smem] + [any_space] * 8...  22.8 us
    ppermute x5, starting transfers between devices, sum_everywhere(): lax.ppermute(value, axis, [(place, place ^ step) for place in range(size)])  9.96 us
    ppermute x5, waiting for transfers between devices, sum_everywhere(): lax.ppermute(value, axis, [(place, place ^ step) for place in range(size)])  8 us
    pallas_call x1, Pallas kernels, pack(): pl.pallas_call(pack_kernel, in_specs=[smem, smem, any_space, any_space],...  4.5 us
  transfers between devices with their start and end apart: 12, of which 5 were waited for; matrix products, arithmetic and copies ran while one was open for 0% of the time, Pallas kernels for 25%

profile of v1, /device:TPU:0, one launch (start us, length us, event | category | flops | bytes accessed | tf_op | source)
XLA Modules:
  0.0 111.1 jit_solution(14148457413862519084)
XLA Ops:
  0.6 0.5 collective-permute-start
  1.2 0.1 collective-permute-start.1
  1.2 0.4 collective-permute-start.2
  1.7 0.1 collective-permute-start.3
  1.7 4.5 %pack_rows.1 = (bf16[1024,768]{1,0:T(8,128)(2,1)}, bf16[1024,768]{1,0:T(8,128)(2,1)}) custom-call(s32[1]{0:T(128)} %bitcast.own_ref, s32[2,8]{1,0:T(2,128)} %len_ref.5, bf16[2048,768]{1,0:T(8,128)(2,1)} %x_hbm.1, bf16[1024,768]{1,0:T(8,128)(2,1)} %grad_hbm.1), custom_call_target="tpu_custom_call" | custom-call | flops 3000000000 | bytes 6000000 | tf_op jit(solution)/shard_map/pack_rows/pallas_call | solution.py:201
  6.2 0.5 collective-permute-start.5
  6.7 0.1 collective-permute-start.6
  6.9 0.4 collective-permute-start.4
  7.3 0.1 copy-done.4
  7.3 22.8 %attention_forward.1 = (bf16[2,6,4,1024,256]{4,3,2,1,0:T(8,128)(2,1)}, bf16[1024,768]{1,0:T(8,128)(2,1)}, bf16[1024,768]{1,0:T(8,128)(2,1)}, bf16[1024,768]{1,0:...) custom-call(s32[1]{0:T(128)} %bitcast.own_ref, s32[2,8]{1,0:T(2,128)} %len_ref.5, ...), custom_call_target="tpu_custom_call" | custom-call | flops 24999999488 | bytes 30000000 | tf_op jit(solution)/shard_map/attention_forward/pallas_call | solution.py:398
  30.2 0.0 copy-start.2
  30.2 61.5 %feed_forward_and_back.1 = (f32[1024,768]{1,0:T(8,128)}, f32[1024,768]{1,0:T(8,128)}, f32[2512]{0:T(1024)}) custom-call(s32[1]{0:T(128)} %bitcast.own_ref, s32[2,8]{1,0:T(2,128)} %len_ref.5, bf16[2,6,4,1024,256]{4,3,2,1,0:T(8,128)(2,1)} %get-tuple-element.21.prob_hbm, bf16[1024,768]{1,0:T(8,128)(2,1)} %get-tuple-element.22.q_hbm, ...), custom_call_target="tpu_custom_call" | custom-call | flops 60000002048 | bytes 40000000 | tf_op jit(solution)/shard_map/feed_forward_and_back/pallas_call | solution.py:825
  91.7 0.1 collective-permute-start.7
  91.9 1.3 %collective-permute-done.7 = f32[2512]{0:T(1024)S(1)} collective-permute-done((f32[2512]{0:T(1024)}, f32[2512]{0:T(1024)S(1)}, u32[]{:S(2)}, u32[]{:S(2)}) %collective-permute-start.7) | collective-permute-done | bytes 10080 | tf_op jit(solution)/shard_map/ppermute | solution.py:864
  93.2 0.7 add.33
  93.9 2.7 %collective-permute-start.8 = (f32[2512]{0:T(1024)S(1)}, f32[2512]{0:T(1024)S(1)}, u32[]{:S(2)}, u32[]{:S(2)}) collective-permute-start(f32[2512]{0:T(1024)S(1)} %add.33), channel_id=1, source_target_pairs={{0,2},{2,0},{4,6},{6,4},{8,10},{10,8},{12,14},{14,12},{16,18},{18,... | collective-permute-start | bytes 30152 | tf_op jit(solution)/shard_map/ppermute | solution.py:864
  96.6 1.7 %collective-permute-done.8 = f32[2512]{0:T(1024)S(1)} collective-permute-done((f32[2512]{0:T(1024)S(1)}, f32[2512]{0:T(1024)S(1)}, u32[]{:S(2)}, u32[]{:S(2)}) %collective-permute-start.8) | collective-permute-done | bytes 10080 | tf_op jit(solution)/shard_map/ppermute | solution.py:864
  98.2 2.0 %collective-permute-start.9 = (f32[2512]{0:T(1024)S(1)}, f32[2512]{0:T(1024)S(1)}, u32[]{:S(2)}, u32[]{:S(2)}) collective-permute-start(f32[2512]{0:T(1024)S(1)} %add.34), channel_id=1, source_target_pairs={{0,4},{2,6},{4,0},{6,2},{8,12},{10,14},{12,8},{14,10},{16,20},{18,... | collective-permute-start | bytes 30152 | tf_op jit(solution)/shard_map/ppermute | solution.py:864
  100.3 1.7 %collective-permute-done.9 = f32[2512]{0:T(1024)S(1)} collective-permute-done((f32[2512]{0:T(1024)S(1)}, f32[2512]{0:T(1024)S(1)}, u32[]{:S(2)}, u32[]{:S(2)}) %collective-permute-start.9) | collective-permute-done | bytes 10080 | tf_op jit(solution)/shard_map/ppermute | solution.py:864
  102.0 2.1 %collective-permute-start.10 = (f32[2512]{0:T(1024)S(1)}, f32[2512]{0:T(1024)S(1)}, u32[]{:S(2)}, u32[]{:S(2)}) collective-permute-start(f32[2512]{0:T(1024)S(1)} %add.35), channel_id=1, source_target_pairs={{0,8},{2,10},{4,12},{6,14},{8,0},{10,2},{12,4},{14,6},{16,24},{18,... | collective-permute-start | bytes 30152 | tf_op jit(solution)/shard_map/ppermute | solution.py:864
  104.0 1.7 %collective-permute-done.10 = f32[2512]{0:T(1024)S(1)} collective-permute-done((f32[2512]{0:T(1024)S(1)}, f32[2512]{0:T(1024)S(1)}, u32[]{:S(2)}, u32[]{:S(2)}) %collective-permute-start.10) | collective-permute-done | bytes 10080 | tf_op jit(solution)/shard_map/ppermute | solution.py:864
  105.7 3.0 %collective-permute-start.11 = (f32[2512]{0:T(1024)S(1)}, f32[2512]{0:T(1024)S(1)}, u32[]{:S(2)}, u32[]{:S(2)}) collective-permute-start(f32[2512]{0:T(1024)S(1)} %add.36), channel_id=1, source_target_pairs={{0,16},{2,18},{4,20},{6,22},{8,24},{10,26},{12,28},{14,30},{16,0},... | collective-permute-start | bytes 30152 | tf_op jit(solution)/shard_map/ppermute | solution.py:864
  108.8 1.7 %collective-permute-done.11 = f32[2512]{0:T(1024)S(1)} collective-permute-done((f32[2512]{0:T(1024)S(1)}, f32[2512]{0:T(1024)S(1)}, u32[]{:S(2)}, u32[]{:S(2)}) %collective-permute-start.11) | collective-permute-done | bytes 10080 | tf_op jit(solution)/shard_map/ppermute | solution.py:864
  110.4 0.6 multiply_add_fusion
  (18 shorter events, 0.1 us)
Async XLA Ops:
  0.6 6.2 %collective-permute-start = (bf16[768,384]{1,0:T(8,128)(2,1)}, bf16[768,384]{1,0:T(8,128)(2,1)}, u32[]{:S(2)}, u32[]{:S(2)}) collective-permute-start(bf16[768,384]{1,0:T(8,128)(2,1)} %wq_own.3), channel_id=1, source_target_pairs={{0,1},{1,0},{2,3},{3,2},{4,5},{5,4},{6,7},{7,6},{8,9},{9,8},{10,11... | collective-permute-start | bytes 1769480 | tf_op jit(solution)/shard_map/ppermute | solution.py:892
  1.2 6.1 %collective-permute-start.1 = (bf16[768,384]{1,0:T(8,128)(2,1)}, bf16[768,384]{1,0:T(8,128)(2,1)}, u32[]{:S(2)}, u32[]{:S(2)}) collective-permute-start(bf16[768,384]{1,0:T(8,128)(2,1)} %wk_own.3), channel_id=1, source_target_pairs={{0,1},{1,0},{2,3},{3,2},{4,5},{5,4},{6,7},{7,6},{8,9},{9,8},{10,11... | collective-permute-start | bytes 1769480 | tf_op jit(solution)/shard_map/ppermute | solution.py:892
  1.2 6.0 %collective-permute-start.2 = (bf16[768,384]{1,0:T(8,128)(2,1)}, bf16[768,384]{1,0:T(8,128)(2,1)}, u32[]{:S(2)}, u32[]{:S(2)}) collective-permute-start(bf16[768,384]{1,0:T(8,128)(2,1)} %wv_own.3), channel_id=1, source_target_pairs={{0,1},{1,0},{2,3},{3,2},{4,5},{5,4},{6,7},{7,6},{8,9},{9,8},{10,11... | collective-permute-start | bytes 1769480 | tf_op jit(solution)/shard_map/ppermute | solution.py:892
  1.7 5.1 %collective-permute-start.3 = (f32[6,32]{1,0:T(8,128)}, f32[6,32]{1,0:T(8,128)S(1)}, u32[]{:S(2)}, u32[]{:S(2)}) collective-permute-start(f32[6,32]{1,0:T(8,128)} %bitcast.2), channel_id=1, source_target_pairs={{0,1},{1,0},{2,3},{3,2},{4,5},{5,4},{6,7},{7,6},{8,9},{9,8},{10,11... | collective-permute-start | bytes 2312 | tf_op jit(solution)/shard_map/ppermute | solution.py:892
  6.2 23.9 %collective-permute-start.5 = (bf16[768,1536]{1,0:T(8,128)(2,1)}, bf16[768,1536]{1,0:T(8,128)(2,1)}, u32[]{:S(2)}, u32[]{:S(2)}) collective-permute-start(bf16[768,1536]{1,0:T(8,128)(2,1)} %win_own), channel_id=1, source_target_pairs={{0,1},{1,0},{2,3},{3,2},{4,5},{5,4},{6,7},{7,6},{8,9},{9,8},{10,11... | collective-permute-start | bytes 7077896 | tf_op jit(solution)/shard_map/ppermute | solution.py:892
  6.7 0.6 copy-start.4
  6.7 23.4 %collective-permute-start.6 = (bf16[1536,768]{1,0:T(8,128)(2,1)}, bf16[1536,768]{1,0:T(8,128)(2,1)}, u32[]{:S(2)}, u32[]{:S(2)}) collective-permute-start(bf16[1536,768]{1,0:T(8,128)(2,1)} %wout_own), channel_id=1, source_target_pairs={{0,1},{1,0},{2,3},{3,2},{4,5},{5,4},{6,7},{7,6},{8,9},{9,8},{10,11... | collective-permute-start | bytes 7077896 | tf_op jit(solution)/shard_map/ppermute | solution.py:892
  6.9 23.3 %collective-permute-start.4 = (bf16[384,768]{1,0:T(8,128)(2,1)}, bf16[384,768]{1,0:T(8,128)(2,1)}, u32[]{:S(2)}, u32[]{:S(2)}) collective-permute-start(bf16[384,768]{1,0:T(8,128)(2,1)} %wo_own), channel_id=1, source_target_pairs={{0,1},{1,0},{2,3},{3,2},{4,5},{5,4},{6,7},{7,6},{8,9},{9,8},{10,11... | collective-permute-start | bytes 1769480 | tf_op jit(solution)/shard_map/ppermute | solution.py:892
  30.2 80.3 %copy-start = (f32[2512]{0:T(1024)S(1)}, f32[2512]{0:T(1024)}, u32[]{:S(2)}) copy-start(f32[2512]{0:T(1024)} %flat_ref.1) | copy-start | bytes 30148
  30.2 80.3 %copy-start.1 = (f32[2512]{0:T(1024)S(1)}, f32[2512]{0:T(1024)}, u32[]{:S(2)}) copy-start(f32[2512]{0:T(1024)} %param.33) | copy-start | bytes 30148
  30.2 80.2 %copy-start.2 = (f32[2512]{0:T(1024)S(1)}, f32[2512]{0:T(1024)}, u32[]{:S(2)}) copy-start(f32[2512]{0:T(1024)} %param.31) | copy-start | bytes 30148
  30.2 80.2 %copy-start.3 = (f32[2512]{0:T(1024)S(1)}, f32[2512]{0:T(1024)}, u32[]{:S(2)}) copy-start(f32[2512]{0:T(1024)} %param.32) | copy-start | bytes 30148
  91.7 1.5 %collective-permute-start.7 = (f32[2512]{0:T(1024)}, f32[2512]{0:T(1024)S(1)}, u32[]{:S(2)}, u32[]{:S(2)}) collective-permute-start(f32[2512]{0:T(1024)} %get-tuple-element.33), channel_id=1, source_target_pairs={{0,1},{1,0},{2,3},{3,2},{4,5},{5,4},{6,7},{7,6},{8,9},{9,8},{10,11... | collective-permute-start | bytes 30152 | tf_op jit(solution)/shard_map/ppermute | solution.py:864
  93.9 4.3 %collective-permute-start.8 = (f32[2512]{0:T(1024)S(1)}, f32[2512]{0:T(1024)S(1)}, u32[]{:S(2)}, u32[]{:S(2)}) collective-permute-start(f32[2512]{0:T(1024)S(1)} %add.33), channel_id=1, source_target_pairs={{0,2},{2,0},{4,6},{6,4},{8,10},{10,8},{12,14},{14,12},{16,18},{18,... | collective-permute-start | bytes 30152 | tf_op jit(solution)/shard_map/ppermute | solution.py:864
  98.2 3.7 %collective-permute-start.9 = (f32[2512]{0:T(1024)S(1)}, f32[2512]{0:T(1024)S(1)}, u32[]{:S(2)}, u32[]{:S(2)}) collective-permute-start(f32[2512]{0:T(1024)S(1)} %add.34), channel_id=1, source_target_pairs={{0,4},{2,6},{4,0},{6,2},{8,12},{10,14},{12,8},{14,10},{16,20},{18,... | collective-permute-start | bytes 30152 | tf_op jit(solution)/shard_map/ppermute | solution.py:864
  102.0 3.8 %collective-permute-start.10 = (f32[2512]{0:T(1024)S(1)}, f32[2512]{0:T(1024)S(1)}, u32[]{:S(2)}, u32[]{:S(2)}) collective-permute-start(f32[2512]{0:T(1024)S(1)} %add.35), channel_id=1, source_target_pairs={{0,8},{2,10},{4,12},{6,14},{8,0},{10,2},{12,4},{14,6},{16,24},{18,... | collective-permute-start | bytes 30152 | tf_op jit(solution)/shard_map/ppermute | solution.py:864
  105.7 4.7 %collective-permute-start.11 = (f32[2512]{0:T(1024)S(1)}, f32[2512]{0:T(1024)S(1)}, u32[]{:S(2)}, u32[]{:S(2)}) collective-permute-start(f32[2512]{0:T(1024)S(1)} %add.36), channel_id=1, source_target_pairs={{0,16},{2,18},{4,20},{6,22},{8,24},{10,26},{12,28},{14,30},{16,0},... | collective-permute-start | bytes 30152 | tf_op jit(solution)/shard_map/ppermute | solution.py:864

commit v2 on v1

--- a/solution.py
+++ b/solution.py
@@ -688,21 +688,8 @@
     mixed_grad = (out_grad_low.astype(f32) + nn(bottle_grad, down)).astype(bf16)
     up_grad = tn(bottle_low, out_grad_low)
     down_grad = tn(bottle_grad, mixed_low)
-    core_down, right_down, left_down = down_maker.gradient(down_grad)
-    core_up, left_up, right_up = up_maker.gradient(up_grad)
-    flat_grad = jnp.concatenate(
-        [
-            core_down + core_up,
-            left_down,
-            right_down,
-            left_up,
-            right_up,
-            jnp.sum(bottle_grad.astype(f32), axis=0, keepdims=True),
-            jnp.sum(out_grad_low.astype(f32), axis=0, keepdims=True),
-        ],
-        axis=1,
-    )
-    flat_grad_ref[...] = flat_grad.reshape(flat_grad_ref.shape[0])
+    bias_down_grad = jnp.sum(bottle_grad.astype(f32), axis=0, keepdims=True)
+    bias_up_grad = jnp.sum(out_grad_low.astype(f32), axis=0, keepdims=True)
     low_ref[...] = mixed_grad
     sums_ref[...] = jnp.zeros_like(sums_ref)
 
@@ -732,6 +719,21 @@
     spread = (head_row == head_lane).astype(bf16)
     shrink_wide = tn(shrink_top, spread) + tn(shrink_rest, spread)
     dctx = (nt(res_grad.astype(bf16), wo_ref[...]) * shrink_wide).astype(bf16)
+    core_down, right_down, left_down = down_maker.gradient(down_grad)
+    core_up, left_up, right_up = up_maker.gradient(up_grad)
+    flat_grad = jnp.concatenate(
+        [
+            core_down + core_up,
+            left_down,
+            right_down,
+            left_up,
+            right_up,
+            bias_down_grad,
+            bias_up_grad,
+        ],
+        axis=1,
+    )
+    flat_grad_ref[...] = flat_grad.reshape(flat_grad_ref.shape[0])
     grad_ref[...] = dctx
     product = dctx.T.astype(f32) * ctx_ref[...].astype(f32)
     delta_ref[0 : 2 * heads, :] = jnp.sum(product.reshape(2 * heads, DH, SEQ), axis=1)

time: 111 us -> 111 us (level)
  no operation moved by 1% of the time
where the time goes in v2:
time: 111 us
  Pallas kernels  88.7 us (80%)
  starting transfers between devices  12.1 us (11%)
  waiting for transfers between devices  8.01 us (7%)
  other arithmetic  1.36 us (1%)
    pallas_call x1, Pallas kernels, feed_forward_and_back(): pl.pallas_call(feed_forward_kernel, in_specs=[smem, smem] + [any_space] *...  61.4 us
    pallas_call x1, Pallas kernels, attention_forward(): pl.pallas_call(attention_kernel, in_specs=[smem, smem] + [any_space] * 8...  22.8 us
    ppermute x5, starting transfers between devices, sum_everywhere(): lax.ppermute(value, axis, [(place, place ^ step) for place in range(size)])  9.96 us
    ppermute x5, waiting for transfers between devices, sum_everywhere(): lax.ppermute(value, axis, [(place, place ^ step) for place in range(size)])  8 us
    pallas_call x1, Pallas kernels, pack(): pl.pallas_call(pack_kernel, in_specs=[smem, smem, any_space, any_space],...  4.5 us
  transfers between devices with their start and end apart: 12, of which 5 were waited for; matrix products, arithmetic and copies ran while one was open for 0% of the time, Pallas kernels for 25%

profile of v2, /device:TPU:0, one launch (start us, length us, event | category | flops | bytes accessed | tf_op | source)
XLA Modules:
  0.0 110.9 jit_solution(9092730159269342726)
XLA Ops:
  0.6 0.5 collective-permute-start
  1.2 0.1 collective-permute-start.1
  1.2 0.4 collective-permute-start.2
  1.7 0.1 collective-permute-start.3
  1.7 4.5 %pack_rows.1 = (bf16[1024,768]{1,0:T(8,128)(2,1)}, bf16[1024,768]{1,0:T(8,128)(2,1)}) custom-call(s32[1]{0:T(128)} %bitcast.own_ref, s32[2,8]{1,0:T(2,128)} %len_ref.5, bf16[2048,768]{1,0:T(8,128)(2,1)} %x_hbm.1, bf16[1024,768]{1,0:T(8,128)(2,1)} %grad_hbm.1), custom_call_target="tpu_custom_call" | custom-call | flops 3000000000 | bytes 6000000 | tf_op jit(solution)/shard_map/pack_rows/pallas_call | solution.py:201
  6.2 0.5 collective-permute-start.5
  6.7 0.1 collective-permute-start.6
  6.9 0.4 collective-permute-start.4
  7.3 0.1 copy-done.4
  7.3 22.8 %attention_forward.1 = (bf16[2,6,4,1024,256]{4,3,2,1,0:T(8,128)(2,1)}, bf16[1024,768]{1,0:T(8,128)(2,1)}, bf16[1024,768]{1,0:T(8,128)(2,1)}, bf16[1024,768]{1,0:...) custom-call(s32[1]{0:T(128)} %bitcast.own_ref, s32[2,8]{1,0:T(2,128)} %len_ref.5, ...), custom_call_target="tpu_custom_call" | custom-call | flops 24999999488 | bytes 30000000 | tf_op jit(solution)/shard_map/attention_forward/pallas_call | solution.py:398
  30.2 0.0 copy-start.2
  30.2 61.4 %feed_forward_and_back.1 = (f32[1024,768]{1,0:T(8,128)}, f32[1024,768]{1,0:T(8,128)}, f32[2512]{0:T(1024)}) custom-call(s32[1]{0:T(128)} %bitcast.own_ref, s32[2,8]{1,0:T(2,128)} %len_ref.5, bf16[2,6,4,1024,256]{4,3,2,1,0:T(8,128)(2,1)} %get-tuple-element.21.prob_hbm, bf16[1024,768]{1,0:T(8,128)(2,1)} %get-tuple-element.22.q_hbm, ...), custom_call_target="tpu_custom_call" | custom-call | flops 60000002048 | bytes 40000000 | tf_op jit(solution)/shard_map/feed_forward_and_back/pallas_call | solution.py:827
  91.6 0.1 collective-permute-start.7
  91.7 1.3 %collective-permute-done.7 = f32[2512]{0:T(1024)S(1)} collective-permute-done((f32[2512]{0:T(1024)}, f32[2512]{0:T(1024)S(1)}, u32[]{:S(2)}, u32[]{:S(2)}) %collective-permute-start.7) | collective-permute-done | bytes 10080 | tf_op jit(solution)/shard_map/ppermute | solution.py:866
  93.0 0.7 add.33
  93.8 2.7 %collective-permute-start.8 = (f32[2512]{0:T(1024)S(1)}, f32[2512]{0:T(1024)S(1)}, u32[]{:S(2)}, u32[]{:S(2)}) collective-permute-start(f32[2512]{0:T(1024)S(1)} %add.33), channel_id=1, source_target_pairs={{0,2},{2,0},{4,6},{6,4},{8,10},{10,8},{12,14},{14,12},{16,18},{18,... | collective-permute-start | bytes 30152 | tf_op jit(solution)/shard_map/ppermute | solution.py:866
  96.4 1.7 %collective-permute-done.8 = f32[2512]{0:T(1024)S(1)} collective-permute-done((f32[2512]{0:T(1024)S(1)}, f32[2512]{0:T(1024)S(1)}, u32[]{:S(2)}, u32[]{:S(2)}) %collective-permute-start.8) | collective-permute-done | bytes 10080 | tf_op jit(solution)/shard_map/ppermute | solution.py:866
  98.1 2.0 %collective-permute-start.9 = (f32[2512]{0:T(1024)S(1)}, f32[2512]{0:T(1024)S(1)}, u32[]{:S(2)}, u32[]{:S(2)}) collective-permute-start(f32[2512]{0:T(1024)S(1)} %add.34), channel_id=1, source_target_pairs={{0,4},{2,6},{4,0},{6,2},{8,12},{10,14},{12,8},{14,10},{16,20},{18,... | collective-permute-start | bytes 30152 | tf_op jit(solution)/shard_map/ppermute | solution.py:866
  100.1 1.7 %collective-permute-done.9 = f32[2512]{0:T(1024)S(1)} collective-permute-done((f32[2512]{0:T(1024)S(1)}, f32[2512]{0:T(1024)S(1)}, u32[]{:S(2)}, u32[]{:S(2)}) %collective-permute-start.9) | collective-permute-done | bytes 10080 | tf_op jit(solution)/shard_map/ppermute | solution.py:866
  101.8 2.1 %collective-permute-start.10 = (f32[2512]{0:T(1024)S(1)}, f32[2512]{0:T(1024)S(1)}, u32[]{:S(2)}, u32[]{:S(2)}) collective-permute-start(f32[2512]{0:T(1024)S(1)} %add.35), channel_id=1, source_target_pairs={{0,8},{2,10},{4,12},{6,14},{8,0},{10,2},{12,4},{14,6},{16,24},{18,... | collective-permute-start | bytes 30152 | tf_op jit(solution)/shard_map/ppermute | solution.py:866
  103.9 1.7 %collective-permute-done.10 = f32[2512]{0:T(1024)S(1)} collective-permute-done((f32[2512]{0:T(1024)S(1)}, f32[2512]{0:T(1024)S(1)}, u32[]{:S(2)}, u32[]{:S(2)}) %collective-permute-start.10) | collective-permute-done | bytes 10080 | tf_op jit(solution)/shard_map/ppermute | solution.py:866
  105.6 3.0 %collective-permute-start.11 = (f32[2512]{0:T(1024)S(1)}, f32[2512]{0:T(1024)S(1)}, u32[]{:S(2)}, u32[]{:S(2)}) collective-permute-start(f32[2512]{0:T(1024)S(1)} %add.36), channel_id=1, source_target_pairs={{0,16},{2,18},{4,20},{6,22},{8,24},{10,26},{12,28},{14,30},{16,0},... | collective-permute-start | bytes 30152 | tf_op jit(solution)/shard_map/ppermute | solution.py:866
  108.6 1.7 %collective-permute-done.11 = f32[2512]{0:T(1024)S(1)} collective-permute-done((f32[2512]{0:T(1024)S(1)}, f32[2512]{0:T(1024)S(1)}, u32[]{:S(2)}, u32[]{:S(2)}) %collective-permute-start.11) | collective-permute-done | bytes 10080 | tf_op jit(solution)/shard_map/ppermute | solution.py:866
  110.3 0.6 multiply_add_fusion
  (18 shorter events, 0.1 us)
Async XLA Ops:
  0.6 6.2 %collective-permute-start = (bf16[768,384]{1,0:T(8,128)(2,1)}, bf16[768,384]{1,0:T(8,128)(2,1)}, u32[]{:S(2)}, u32[]{:S(2)}) collective-permute-start(bf16[768,384]{1,0:T(8,128)(2,1)} %wq_own.3), channel_id=1, source_target_pairs={{0,1},{1,0},{2,3},{3,2},{4,5},{5,4},{6,7},{7,6},{8,9},{9,8},{10,11... | collective-permute-start | bytes 1769480 | tf_op jit(solution)/shard_map/ppermute | solution.py:894
  1.2 6.1 %collective-permute-start.1 = (bf16[768,384]{1,0:T(8,128)(2,1)}, bf16[768,384]{1,0:T(8,128)(2,1)}, u32[]{:S(2)}, u32[]{:S(2)}) collective-permute-start(bf16[768,384]{1,0:T(8,128)(2,1)} %wk_own.3), channel_id=1, source_target_pairs={{0,1},{1,0},{2,3},{3,2},{4,5},{5,4},{6,7},{7,6},{8,9},{9,8},{10,11... | collective-permute-start | bytes 1769480 | tf_op jit(solution)/shard_map/ppermute | solution.py:894
  1.2 6.0 %collective-permute-start.2 = (bf16[768,384]{1,0:T(8,128)(2,1)}, bf16[768,384]{1,0:T(8,128)(2,1)}, u32[]{:S(2)}, u32[]{:S(2)}) collective-permute-start(bf16[768,384]{1,0:T(8,128)(2,1)} %wv_own.3), channel_id=1, source_target_pairs={{0,1},{1,0},{2,3},{3,2},{4,5},{5,4},{6,7},{7,6},{8,9},{9,8},{10,11... | collective-permute-start | bytes 1769480 | tf_op jit(solution)/shard_map/ppermute | solution.py:894
  1.7 5.1 %collective-permute-start.3 = (f32[6,32]{1,0:T(8,128)}, f32[6,32]{1,0:T(8,128)S(1)}, u32[]{:S(2)}, u32[]{:S(2)}) collective-permute-start(f32[6,32]{1,0:T(8,128)} %bitcast.2), channel_id=1, source_target_pairs={{0,1},{1,0},{2,3},{3,2},{4,5},{5,4},{6,7},{7,6},{8,9},{9,8},{10,11... | collective-permute-start | bytes 2312 | tf_op jit(solution)/shard_map/ppermute | solution.py:894
  6.2 23.9 %collective-permute-start.5 = (bf16[768,1536]{1,0:T(8,128)(2,1)}, bf16[768,1536]{1,0:T(8,128)(2,1)}, u32[]{:S(2)}, u32[]{:S(2)}) collective-permute-start(bf16[768,1536]{1,0:T(8,128)(2,1)} %win_own), channel_id=1, source_target_pairs={{0,1},{1,0},{2,3},{3,2},{4,5},{5,4},{6,7},{7,6},{8,9},{9,8},{10,11... | collective-permute-start | bytes 7077896 | tf_op jit(solution)/shard_map/ppermute | solution.py:894
  6.7 0.6 copy-start.4
  6.7 23.4 %collective-permute-start.6 = (bf16[1536,768]{1,0:T(8,128)(2,1)}, bf16[1536,768]{1,0:T(8,128)(2,1)}, u32[]{:S(2)}, u32[]{:S(2)}) collective-permute-start(bf16[1536,768]{1,0:T(8,128)(2,1)} %wout_own), channel_id=1, source_target_pairs={{0,1},{1,0},{2,3},{3,2},{4,5},{5,4},{6,7},{7,6},{8,9},{9,8},{10,11... | collective-permute-start | bytes 7077896 | tf_op jit(solution)/shard_map/ppermute | solution.py:894
  6.9 23.3 %collective-permute-start.4 = (bf16[384,768]{1,0:T(8,128)(2,1)}, bf16[384,768]{1,0:T(8,128)(2,1)}, u32[]{:S(2)}, u32[]{:S(2)}) collective-permute-start(bf16[384,768]{1,0:T(8,128)(2,1)} %wo_own), channel_id=1, source_target_pairs={{0,1},{1,0},{2,3},{3,2},{4,5},{5,4},{6,7},{7,6},{8,9},{9,8},{10,11... | collective-permute-start | bytes 1769480 | tf_op jit(solution)/shard_map/ppermute | solution.py:894
  30.2 80.1 %copy-start = (f32[2512]{0:T(1024)S(1)}, f32[2512]{0:T(1024)}, u32[]{:S(2)}) copy-start(f32[2512]{0:T(1024)} %flat_ref.1) | copy-start | bytes 30148
  30.2 80.1 %copy-start.1 = (f32[2512]{0:T(1024)S(1)}, f32[2512]{0:T(1024)}, u32[]{:S(2)}) copy-start(f32[2512]{0:T(1024)} %param.33) | copy-start | bytes 30148
  30.2 80.1 %copy-start.2 = (f32[2512]{0:T(1024)S(1)}, f32[2512]{0:T(1024)}, u32[]{:S(2)}) copy-start(f32[2512]{0:T(1024)} %param.31) | copy-start | bytes 30148
  30.2 80.1 %copy-start.3 = (f32[2512]{0:T(1024)S(1)}, f32[2512]{0:T(1024)}, u32[]{:S(2)}) copy-start(f32[2512]{0:T(1024)} %param.32) | copy-start | bytes 30148
  91.6 1.5 %collective-permute-start.7 = (f32[2512]{0:T(1024)}, f32[2512]{0:T(1024)S(1)}, u32[]{:S(2)}, u32[]{:S(2)}) collective-permute-start(f32[2512]{0:T(1024)} %get-tuple-element.33), channel_id=1, source_target_pairs={{0,1},{1,0},{2,3},{3,2},{4,5},{5,4},{6,7},{7,6},{8,9},{9,8},{10,11... | collective-permute-start | bytes 30152 | tf_op jit(solution)/shard_map/ppermute | solution.py:866
  93.8 4.3 %collective-permute-start.8 = (f32[2512]{0:T(1024)S(1)}, f32[2512]{0:T(1024)S(1)}, u32[]{:S(2)}, u32[]{:S(2)}) collective-permute-start(f32[2512]{0:T(1024)S(1)} %add.33), channel_id=1, source_target_pairs={{0,2},{2,0},{4,6},{6,4},{8,10},{10,8},{12,14},{14,12},{16,18},{18,... | collective-permute-start | bytes 30152 | tf_op jit(solution)/shard_map/ppermute | solution.py:866
  98.1 3.7 %collective-permute-start.9 = (f32[2512]{0:T(1024)S(1)}, f32[2512]{0:T(1024)S(1)}, u32[]{:S(2)}, u32[]{:S(2)}) collective-permute-start(f32[2512]{0:T(1024)S(1)} %add.34), channel_id=1, source_target_pairs={{0,4},{2,6},{4,0},{6,2},{8,12},{10,14},{12,8},{14,10},{16,20},{18,... | collective-permute-start | bytes 30152 | tf_op jit(solution)/shard_map/ppermute | solution.py:866
  101.8 3.8 %collective-permute-start.10 = (f32[2512]{0:T(1024)S(1)}, f32[2512]{0:T(1024)S(1)}, u32[]{:S(2)}, u32[]{:S(2)}) collective-permute-start(f32[2512]{0:T(1024)S(1)} %add.35), channel_id=1, source_target_pairs={{0,8},{2,10},{4,12},{6,14},{8,0},{10,2},{12,4},{14,6},{16,24},{18,... | collective-permute-start | bytes 30152 | tf_op jit(solution)/shard_map/ppermute | solution.py:866
  105.6 4.7 %collective-permute-start.11 = (f32[2512]{0:T(1024)S(1)}, f32[2512]{0:T(1024)S(1)}, u32[]{:S(2)}, u32[]{:S(2)}) collective-permute-start(f32[2512]{0:T(1024)S(1)} %add.36), channel_id=1, source_target_pairs={{0,16},{2,18},{4,20},{6,22},{8,24},{10,26},{12,28},{14,30},{16,0},... | collective-permute-start | bytes 30152 | tf_op jit(solution)/shard_map/ppermute | solution.py:866
